TPU v7x, 512 devices: a whole 4x8x8 slice. The times are simulated.
512 devices in a mesh: gx: 32 (over x, y), gy: 16 (over z, core).
Axes of the slice: x: 4, y: 8, z: 8, core: 2. Of those that a mesh axis runs over, the one named last changes fastest.
Arguments:
- orbitals: bfloat16 [32, 16, 1, 64, 4096], P('gx', 'gy'), may hold values from -6 to 6
- pair_table: int32 [32, 16, 4, 5], P('gx', 'gy'), may hold values from -32 to 511, as said below
Outputs:
- exchange_terms: float32 [32, 16, 1, 64, 4096], P('gx', 'gy')
Inputs may be any that keep to these rules, and one draw needn't show every extreme that they name: `pair_table`: each device's list holds its live rows first, then empty rows (-1, -1, 0, 0, 0); some device lists exactly 4 live rows. In a live row, orbital i belongs to the listing device; orbital j != i belongs to that device or to one of the eight devices around it in the two axes, wrapping around both axes. Each unordered pair of orbitals is listed at most once overall. Every component of s lies between -32 and 32.
All inputs are finite; a program needn't handle non-finite values.
Results may differ from a plain program's by a relative error of at most 0.00035.
Values may be sent and summed in bfloat16 or wider, within the bound.
A program may use at most 128 MiB of HBM per device.

v0:
```python
import math

import jax
import jax.numpy as jnp
from jax import lax
from jax.sharding import PartitionSpec as P

HIGH = lax.Precision.HIGHEST


def from_behind(block, axis, distance):
    devices = range(lax.axis_size(axis))
    route = [((i - distance) % len(devices), i) for i in devices]
    return lax.ppermute(block, axis, route)


def extended(cells, sides, width):
    for axis, dim in sides:
        count = lax.axis_size(axis)
        head = lax.slice_in_dim(cells, 0, width, axis=dim)
        tail = lax.slice_in_dim(cells, cells.shape[dim] - width, cells.shape[dim], axis=dim)
        cells = jnp.concatenate(
            [
                lax.ppermute(tail, axis, [(i, (i + 1) % count) for i in range(count)]),
                cells,
                lax.ppermute(head, axis, [((i + 1) % count, i) for i in range(count)]),
            ],
            axis=dim,
        )
    return cells


def make_sine(box_len):
    positions = jnp.arange(box_len, dtype=jnp.float32) + 1.0
    return jnp.sin(math.pi * positions[:, None] * positions[None, :] / (box_len + 1))


def inverse_weights(box_len):
    positions = jnp.arange(box_len, dtype=jnp.float32) + 1.0
    eigen_vals = 2.0 - 2.0 * jnp.cos(math.pi * positions / (box_len + 1))
    denominator = eigen_vals[:, None, None] + eigen_vals[None, :, None] + eigen_vals[None, None, :]
    return (2.0 / (box_len + 1)) ** 3 / denominator


def transform(grid_field, sine_table):
    box_len = grid_field.shape[0]
    result = jnp.dot(sine_table, grid_field.reshape(box_len, box_len * box_len), precision=HIGH)
    result = result.reshape(box_len, box_len, box_len)
    result = jnp.einsum("kn,anb->akb", sine_table, result, precision=HIGH)
    return jnp.einsum("kn,abn->abk", sine_table, result, precision=HIGH)


def move_in(box_data, offset_cells):
    half_box = box_data.shape[0] // 2
    padded = jnp.pad(box_data, half_box)
    corner = half_box - offset_cells
    return lax.dynamic_slice(padded, (corner[0], corner[1], corner[2]), box_data.shape)


def move_out(grid_field, offset_cells):
    half_box = grid_field.shape[0] // 2
    padded = jnp.pad(grid_field, half_box)
    corner = half_box + offset_cells
    return lax.dynamic_slice(padded, (corner[0], corner[1], corner[2]), grid_field.shape)


def pair_terms(first_box, second_box, offset_cells, sine_table, weights):
    partner = move_in(second_box, offset_cells).astype(jnp.float32)
    own_values = first_box.astype(jnp.float32)
    density = own_values * partner
    potential = transform(transform(density, sine_table) * weights, sine_table)
    return (-potential * partner, move_out(-potential * own_values, offset_cells))


def send_back(collected):
    column = collected[1] + from_behind(collected[2], "gx", 1) + from_behind(collected[0], "gx", -1)
    return column[1] + from_behind(column[2], "gy", 1) + from_behind(column[0], "gy", -1)


def body(orbitals, pair_table):
    per_device = orbitals.shape[2]
    box_len = orbitals.shape[3]
    here_x = lax.axis_index("gx")
    here_y = lax.axis_index("gy")
    span_x = lax.axis_size("gx")
    span_y = lax.axis_size("gy")
    sine_table = make_sine(box_len)
    weights = inverse_weights(box_len)
    nearby = extended(orbitals, (("gx", 0), ("gy", 1)), 1)
    box_stack = nearby.reshape(9 * per_device, box_len, box_len, box_len)

    def locate(orbital):
        owner_x = orbital // (span_y * per_device)
        owner_y = orbital // per_device % span_y
        box_slot = orbital % per_device
        return ((owner_x - here_x + 1) % span_x, (owner_y - here_y + 1) % span_y, box_slot)

    pair_rows = pair_table.reshape(-1, 5)
    live_count = jnp.sum((pair_rows[:, 0] >= 0).astype(jnp.int32))

    def add_pair(position, running):
        pair_row = lax.dynamic_index_in_dim(pair_rows, position, 0, keepdims=False)
        first_x, first_y, first_box = locate(pair_row[0])
        second_x, second_y, second_box = locate(pair_row[1])
        first_slot = (first_x * 3 + first_y) * per_device + first_box
        second_slot = (second_x * 3 + second_y) * per_device + second_box
        own_term, partner_term = pair_terms(
            box_stack[first_slot], box_stack[second_slot], pair_row[2:5], sine_table, weights
        )
        return running.at[first_slot].add(own_term).at[second_slot].add(partner_term)

    collected = lax.fori_loop(0, live_count, add_pair, jnp.zeros(box_stack.shape, jnp.float32))
    collected = collected.reshape(3, 3, per_device, box_len, box_len * box_len)
    summed = send_back(collected)
    return summed.reshape(orbitals.shape)


def solution(mesh):
    in_specs = (P("gx", "gy", None, None, None), P("gx", "gy", None, None))
    out_specs = P("gx", "gy", None, None, None)
    return jax.shard_map(body, mesh=mesh, in_specs=in_specs, out_specs=out_specs, check_vma=False)
```

profile of v0, /device:TPU:26, one launch (start us, length us, event | category | flops | bytes accessed | tf_op | source)
XLA Modules:
  0.0 441.2 jit_solution(2672383150982468324)
XLA Ops:
  0.0 4.8 %collective-permute-start = (bf16[1,1,1,64,4096]{4,3,2,1,0:T(8,128)(2,1)}, bf16[1,1,1,64,4096]{4,3,2,1,0:T(8,128)(2,1)S(1)}, u32[]{:S(2)}, u32[]{:S(2)}) collective-permute-start(bf16[1,1,1,64,4096]{4,3,2,1,0:T(8,128)(2,1)} %param.8), channel_id=1, source_target_pairs={{0,16},{16,32},{32,48},{48,64},{64,80},{80,96},{96,112},{112,128},... | collective-permute-start | bytes 1572872 | tf_op jit(solution)/shard_map/ppermute | solution.py:24
  4.8 1.9 collective-permute-start.1
  6.8 9.5 %collective-permute-done = bf16[1,1,1,64,4096]{4,3,2,1,0:T(8,128)(2,1)S(1)} collective-permute-done((bf16[1,1,1,64,4096]{4,3,2,1,0:T(8,128)(2,1)}, bf16[1,1,1,64,4096]{4,3,2,1,0:T(8,128)(2,1)S(1)}, u32[]{:S(2)}, u32[]{:S(2)}) %collective-permute-start) | collective-permute-done | bytes 524320 | tf_op jit(solution)/shard_map/ppermute | solution.py:24
  17.4 4.1 collective-permute-done.1
  21.6 7.3 %collective-permute-start.3 = (bf16[3,1,1,64,4096]{4,3,2,1,0:T(8,128)(2,1)S(1)}, bf16[3,1,1,64,4096]{4,3,2,1,0:T(8,128)(2,1)S(1)}, u32[]{:S(2)}, u32[]{:S(2)}) collective-permute-start(bf16[3,1,1,64,4096]{4,3,2,1,0:T(8,128)(2,1)S(1)} %constant_dynamic-update-slice_fusion), channel_id=1, source_target_pairs={{1,0},{2,1},{3,2},{4,3},{5,4},{6,5},{7,6},{8,7},{9,8},{10,9},{11,1... | collective-permute-start | bytes 4718600 | tf_op jit(solution)/shard_map/ppermute | solution.py:26
  29.6 17.2 %collective-permute-done.3 = bf16[3,1,1,64,4096]{4,3,2,1,0:T(8,128)(2,1)S(1)} collective-permute-done((bf16[3,1,1,64,4096]{4,3,2,1,0:T(8,128)(2,1)S(1)}, bf16[3,1,1,64,4096]{4,3,2,1,0:T(8,128)(2,1)S(1)}, u32[]{:S(2)}, u32[]{:S(2)}) %collective-permute-start.3) | collective-permute-done | bytes 1572896 | tf_op jit(solution)/shard_map/ppermute | solution.py:26
  46.8 3.2 collective-permute-done.2
  50.0 3.5 pad_maximum_fusion
  53.5 13.8 %reshape.232 = bf16[9,64,64,64]{3,2,1,0:T(8,128)(2,1)} reshape(bf16[3,3,1,64,4096]{4,3,2,1,0:T(8,128)(2,1)} %pad_maximum_fusion) | data formatting | bytes 9437184 | tf_op jit(solution)/shard_map/reshape | solution.py:90
  67.4 8.9 %broadcast_in_dim.2 = f32[9,64,64,64]{3,2,1,0:T(8,128)} broadcast(f32[]{:T(128)} %constant.254.clone.1), dimensions={} | broadcast | bytes 9437188 | tf_op jit(solution)/shard_map/broadcast_in_dim | solution.py:112
  76.2 126.4 %while.17 = (s32[]{:T(128)}, f32[9,64,64,64]{3,2,1,0:T(8,128)}, s32[]{:T(128)}, s32[4,5]{1,0:T(4,128)S(1)}, s32[]{:T(128)}, /*index=5*/s32[]{:T(128)}, bf16[9,64...) while((s32[]{:T(128)}, f32[9,64,64,64]{3,2,1,0:T(8,128)}, ...), condition=%wide.region_4.5_spmd.clone.clone, body=%wide.region_1.4_spmd.clone.clone.sunk | while | flops 1212203264 | bytes 36723616 | solution.py:112
  97.4 4.5 %convert_multiply_fusion.5 = f32[64,64,64]{2,1,0:T(8,128)S(1)} fusion(bf16[9,64,64,64]{3,2,1,0:T(8,128)(2,1)} %get-tuple-element.473, s32[]{:T(128)} %select_n.218, s32[]{:T(128)S(6)} %select_n.224, s32[]{:T(128)S(6)} %select_n.225, s32[]{:T(128)S(6)} %select_n.226, bf16[64,64,64]{2,1,0:T(8,128)(2,1)S(1)} %dynamic-slice_bitcast_fusion.2), kind=kLoop, calls=%fused_computation.9.clone.1 | loop fusion | flops 786432 | bytes 2097168 | tf_op jit(solution)/shard_map/while/body/mul | solution.py:70
  102.0 1.6 reshape.253
  103.6 3.5 convolution_bitcast_fusion.4
  107.1 2.0 reshape.254
  109.1 2.2 fusion.79
  111.3 3.5 divide_multiply_fusion.2
  114.8 2.1 reshape.255
  116.9 2.3 convolution_bitcast_fusion.5
  119.2 2.0 reshape.256
  121.2 2.2 fusion.80
  123.4 8.3 %fusion.81 = (f32[9,64,64,64]{3,2,1,0:T(8,128)}, f32[64,64,64]{2,1,0:T(8,128)S(1)}) fusion(f32[9,64,64,64]{3,2,1,0:T(8,128)} %get-tuple-element.444, s32[]{:T(128)} %select_n.218, pred[]{:T(512)} %get-tuple-element.407, s32[]{:T(128)S(6)} %select_n.224, s32[]{:T(128)S(6)} %select_n.225, s32[]{:T(128)S(6)} %select_n.226, ...), kind=kOutput, calls=%fused_computation.12.clone.1 | convolution fusion | flops 202645504 | bytes 6817292 | tf_op jit(solution)/shard_map/while/body/kn,abn->abk/dot_general | solution.py:50
  131.8 1.7 convert_multiply_fusion.6
  133.5 5.6 %fusion.82 = f32[9,64,64,64]{3,2,1,0:T(8,128)} fusion(f32[9,64,64,64]{3,2,1,0:T(8,128)} %get-tuple-element.413, s32[]{:T(128)} %select_n.223, s32[]{:T(128)S(6)} %select_n.227, s32[]{:T(128)S(6)} %select_n.228, s32[]{:T(128)S(6)} %select_n.229, f32[64,64,64]{2,1,0:T(8,128)S(1)} %convert_multiply_fusion.6, pred[]{:T(512)} %get-tuple-element.418), kind=kLoop, calls=%fused_computation.13.clone.1 | loop fusion | flops 524288 | bytes 5243916 | tf_op jit(solution)/shard_map/while/body/scatter-add | solution.py:110
  160.1 4.5 %convert_multiply_fusion.5 = f32[64,64,64]{2,1,0:T(8,128)S(1)} fusion(bf16[9,64,64,64]{3,2,1,0:T(8,128)(2,1)} %get-tuple-element.473, s32[]{:T(128)} %select_n.218, s32[]{:T(128)S(6)} %select_n.224, s32[]{:T(128)S(6)} %select_n.225, s32[]{:T(128)S(6)} %select_n.226, bf16[64,64,64]{2,1,0:T(8,128)(2,1)S(1)} %dynamic-slice_bitcast_fusion.2), kind=kLoop, calls=%fused_computation.9.clone.1 | loop fusion | flops 786432 | bytes 2097168 | tf_op jit(solution)/shard_map/while/body/mul | solution.py:70
  164.7 1.6 reshape.253
  166.3 3.5 convolution_bitcast_fusion.4
  169.8 2.0 reshape.254
  171.8 2.2 fusion.79
  174.0 3.5 divide_multiply_fusion.2
  177.5 2.1 reshape.255
  179.7 2.3 convolution_bitcast_fusion.5
  181.9 2.0 reshape.256
  183.9 2.2 fusion.80
  186.1 8.3 %fusion.81 = (f32[9,64,64,64]{3,2,1,0:T(8,128)}, f32[64,64,64]{2,1,0:T(8,128)S(1)}) fusion(f32[9,64,64,64]{3,2,1,0:T(8,128)} %get-tuple-element.444, s32[]{:T(128)} %select_n.218, pred[]{:T(512)} %get-tuple-element.407, s32[]{:T(128)S(6)} %select_n.224, s32[]{:T(128)S(6)} %select_n.225, s32[]{:T(128)S(6)} %select_n.226, ...), kind=kOutput, calls=%fused_computation.12.clone.1 | convolution fusion | flops 202645504 | bytes 6817292 | tf_op jit(solution)/shard_map/while/body/kn,abn->abk/dot_general | solution.py:50
  194.5 1.7 convert_multiply_fusion.6
  196.2 5.7 %fusion.82 = f32[9,64,64,64]{3,2,1,0:T(8,128)} fusion(f32[9,64,64,64]{3,2,1,0:T(8,128)} %get-tuple-element.413, s32[]{:T(128)} %select_n.223, s32[]{:T(128)S(6)} %select_n.227, s32[]{:T(128)S(6)} %select_n.228, s32[]{:T(128)S(6)} %select_n.229, f32[64,64,64]{2,1,0:T(8,128)S(1)} %convert_multiply_fusion.6, pred[]{:T(512)} %get-tuple-element.418), kind=kLoop, calls=%fused_computation.13.clone.1 | loop fusion | flops 524288 | bytes 5243916 | tf_op jit(solution)/shard_map/while/body/scatter-add | solution.py:110
  202.7 12.1 %fusion.50 = (f32[3,64,64,64]{3,2,1,0:T(8,128)}, f32[3,64,64,64]{3,2,1,0:T(8,128)}, f32[3,64,64,64]{3,2,1,0:T(8,128)}) fusion(f32[9,64,64,64]{3,2,1,0:T(8,128)} %get-tuple-element.219), kind=kLoop, calls=%fused_computation.83 | loop fusion | bytes 18874368 | tf_op jit(solution)/shard_map/slice | solution.py:76
  214.8 5.8 %squeeze.90 = f32[3,1,64,4096]{3,2,1,0:T(8,128)} reshape(f32[3,64,64,64]{3,2,1,0:T(8,128)} %get-tuple-element.316) | data formatting | bytes 6291456 | tf_op jit(solution)/shard_map/squeeze | solution.py:76
  220.6 5.8 %squeeze.91 = f32[3,1,64,4096]{3,2,1,0:T(8,128)} reshape(f32[3,64,64,64]{3,2,1,0:T(8,128)} %get-tuple-element.318) | data formatting | bytes 6291456 | tf_op jit(solution)/shard_map/squeeze | solution.py:76
  226.5 1.9 collective-permute-start.5
  228.4 64.4 %collective-permute-start.4 = (f32[3,1,64,4096]{3,2,1,0:T(8,128)}, f32[3,1,64,4096]{3,2,1,0:T(8,128)}, u32[]{:S(2)}, u32[]{:S(2)}) collective-permute-start(f32[3,1,64,4096]{3,2,1,0:T(8,128)} %squeeze.90), channel_id=1, source_target_pairs={{496,0},{0,16},{16,32},{32,48},{48,64},{64,80},{80,96},{96,112},{1... | collective-permute-start | bytes 9437192 | tf_op jit(solution)/shard_map/ppermute | solution.py:14
  292.8 4.5 %squeeze.89 = f32[3,1,64,4096]{3,2,1,0:T(8,128)S(1)} reshape(f32[3,64,64,64]{3,2,1,0:T(8,128)} %get-tuple-element.317) | data formatting | bytes 6291456 | tf_op jit(solution)/shard_map/squeeze | solution.py:76
  297.2 54.5 %collective-permute-done.5 = f32[3,1,64,4096]{3,2,1,0:T(8,128)} collective-permute-done((f32[3,1,64,4096]{3,2,1,0:T(8,128)}, f32[3,1,64,4096]{3,2,1,0:T(8,128)}, u32[]{:S(2)}, u32[]{:S(2)}) %collective-permute-start.5) | collective-permute-done | bytes 3145760 | tf_op jit(solution)/shard_map/ppermute | solution.py:14
  351.7 38.0 %collective-permute-done.4 = f32[3,1,64,4096]{3,2,1,0:T(8,128)} collective-permute-done((f32[3,1,64,4096]{3,2,1,0:T(8,128)}, f32[3,1,64,4096]{3,2,1,0:T(8,128)}, u32[]{:S(2)}, u32[]{:S(2)}) %collective-permute-start.4) | collective-permute-done | bytes 3145760 | tf_op jit(solution)/shard_map/ppermute | solution.py:14
  389.7 3.5 add_add_fusion
  393.3 34.2 %collective-permute-start.7 = (f32[1,64,4096]{2,1,0:T(8,128)S(1)}, f32[1,64,4096]{2,1,0:T(8,128)S(1)}, u32[]{:S(2)}, u32[]{:S(2)}) collective-permute-start(f32[1,64,4096]{2,1,0:T(8,128)S(1)} %get-tuple-element.320), channel_id=1, source_target_pairs={{1,0},{2,1},{3,2},{4,3},{5,4},{6,5},{7,6},{8,7},{9,8},{10,9},{11,1... | collective-permute-start | bytes 3145736 | tf_op jit(solution)/shard_map/ppermute | solution.py:14
  427.5 12.5 %collective-permute-done.6 = f32[1,64,4096]{2,1,0:T(8,128)S(1)} collective-permute-done((f32[1,64,4096]{2,1,0:T(8,128)S(1)}, f32[1,64,4096]{2,1,0:T(8,128)S(1)}, u32[]{:S(2)}, u32[]{:S(2)}) %collective-permute-start.6) | collective-permute-done | bytes 1048608 | tf_op jit(solution)/shard_map/ppermute | solution.py:14
  (28 shorter events, 10.1 us)
Async XLA Ops:
  0.0 28.9 %copy-start.1 = (s32[1,1,4,5]{3,2,1,0:T(4,128)S(1)}, s32[1,1,4,5]{3,2,1,0:T(4,128)}, u32[]{:S(2)}) copy-start(s32[1,1,4,5]{3,2,1,0:T(4,128)} %param.9) | copy-start | bytes 244
  0.0 16.3 %collective-permute-start = (bf16[1,1,1,64,4096]{4,3,2,1,0:T(8,128)(2,1)}, bf16[1,1,1,64,4096]{4,3,2,1,0:T(8,128)(2,1)S(1)}, u32[]{:S(2)}, u32[]{:S(2)}) collective-permute-start(bf16[1,1,1,64,4096]{4,3,2,1,0:T(8,128)(2,1)} %param.8), channel_id=1, source_target_pairs={{0,16},{16,32},{32,48},{48,64},{64,80},{80,96},{96,112},{112,128},... | collective-permute-start | bytes 1572872 | tf_op jit(solution)/shard_map/ppermute | solution.py:24
  4.8 16.7 %collective-permute-start.1 = (bf16[1,1,1,64,4096]{4,3,2,1,0:T(8,128)(2,1)}, bf16[1,1,1,64,4096]{4,3,2,1,0:T(8,128)(2,1)S(1)}, u32[]{:S(2)}, u32[]{:S(2)}) collective-permute-start(bf16[1,1,1,64,4096]{4,3,2,1,0:T(8,128)(2,1)} %param.8), channel_id=1, source_target_pairs={{16,0},{32,16},{48,32},{64,48},{80,64},{96,80},{112,96},{128,112},... | collective-permute-start | bytes 1572872 | tf_op jit(solution)/shard_map/ppermute | solution.py:26
  21.6 25.2 %collective-permute-start.3 = (bf16[3,1,1,64,4096]{4,3,2,1,0:T(8,128)(2,1)S(1)}, bf16[3,1,1,64,4096]{4,3,2,1,0:T(8,128)(2,1)S(1)}, u32[]{:S(2)}, u32[]{:S(2)}) collective-permute-start(bf16[3,1,1,64,4096]{4,3,2,1,0:T(8,128)(2,1)S(1)} %constant_dynamic-update-slice_fusion), channel_id=1, source_target_pairs={{1,0},{2,1},{3,2},{4,3},{5,4},{6,5},{7,6},{8,7},{9,8},{10,9},{11,1... | collective-permute-start | bytes 4718600 | tf_op jit(solution)/shard_map/ppermute | solution.py:26
  28.9 21.2 %collective-permute-start.2 = (bf16[3,1,1,64,4096]{4,3,2,1,0:T(8,128)(2,1)S(1)}, bf16[3,1,1,64,4096]{4,3,2,1,0:T(8,128)(2,1)}, u32[]{:S(2)}, u32[]{:S(2)}) collective-permute-start(bf16[3,1,1,64,4096]{4,3,2,1,0:T(8,128)(2,1)S(1)} %constant_dynamic-update-slice_fusion), channel_id=1, source_target_pairs={{0,1},{1,2},{2,3},{3,4},{4,5},{5,6},{6,7},{7,8},{8,9},{9,10},{10,1... | collective-permute-start | bytes 4718600 | tf_op jit(solution)/shard_map/ppermute | solution.py:24
  67.4 8.9 %copy-start = (s32[4]{0:T(128)S(1)}, s32[4]{0:T(128)}, u32[]{:S(2)}) copy-start(s32[4]{0:T(128)} %constant.248.clone.3) | copy-start | bytes 52
  226.5 125.3 %collective-permute-start.5 = (f32[3,1,64,4096]{3,2,1,0:T(8,128)}, f32[3,1,64,4096]{3,2,1,0:T(8,128)}, u32[]{:S(2)}, u32[]{:S(2)}) collective-permute-start(f32[3,1,64,4096]{3,2,1,0:T(8,128)} %squeeze.91), channel_id=1, source_target_pairs={{16,0},{32,16},{48,32},{64,48},{80,64},{96,80},{112,96},{128,112},... | collective-permute-start | bytes 9437192 | tf_op jit(solution)/shard_map/ppermute | solution.py:14
  228.4 161.3 %collective-permute-start.4 = (f32[3,1,64,4096]{3,2,1,0:T(8,128)}, f32[3,1,64,4096]{3,2,1,0:T(8,128)}, u32[]{:S(2)}, u32[]{:S(2)}) collective-permute-start(f32[3,1,64,4096]{3,2,1,0:T(8,128)} %squeeze.90), channel_id=1, source_target_pairs={{496,0},{0,16},{16,32},{32,48},{48,64},{64,80},{80,96},{96,112},{1... | collective-permute-start | bytes 9437192 | tf_op jit(solution)/shard_map/ppermute | solution.py:14
  393.3 46.7 %collective-permute-start.6 = (f32[1,64,4096]{2,1,0:T(8,128)S(1)}, f32[1,64,4096]{2,1,0:T(8,128)S(1)}, u32[]{:S(2)}, u32[]{:S(2)}) collective-permute-start(f32[1,64,4096]{2,1,0:T(8,128)S(1)} %get-tuple-element.319), channel_id=1, source_target_pairs={{15,0},{0,1},{1,2},{2,3},{3,4},{4,5},{5,6},{6,7},{7,8},{8,9},{9,10... | collective-permute-start | bytes 3145736 | tf_op jit(solution)/shard_map/ppermute | solution.py:14
  393.3 46.7 %collective-permute-start.7 = (f32[1,64,4096]{2,1,0:T(8,128)S(1)}, f32[1,64,4096]{2,1,0:T(8,128)S(1)}, u32[]{:S(2)}, u32[]{:S(2)}) collective-permute-start(f32[1,64,4096]{2,1,0:T(8,128)S(1)} %get-tuple-element.320), channel_id=1, source_target_pairs={{1,0},{2,1},{3,2},{4,3},{5,4},{6,5},{7,6},{8,7},{9,8},{10,9},{11,1... | collective-permute-start | bytes 3145736 | tf_op jit(solution)/shard_map/ppermute | solution.py:14
where the time goes:
time: 446 us; the launch traced here: 441 us
  waiting for transfers between devices  139 us (31%)
  starting transfers between devices  115 us (26%)
  local copies, waits for them, and re-layouts  72.9 us (16%)
  matrix products  44 us (10%)
  loops' own time  36.2 us (8%)
  other arithmetic  34.5 us (8%)
    ppermute x4, waiting for transfers between devices, from_behind(): return lax.ppermute(block, axis, route)  105 us
    ppermute x4, starting transfers between devices, from_behind(): return lax.ppermute(block, axis, route)  101 us
    another operation x1, loops' own time, body(): lax.fori_loop(0, live_count, add_pair, jnp.zeros(box_stack.shape, jnp.flo...  36.2 us
    dot_general x4, matrix products, transform(): return jnp.einsum('kn,abn->abk', sine_table, result, precision=HIGH)  23.6 us
    ppermute x2, waiting for transfers between devices, extended(): lax.ppermute(head, axis, [((i + 1) % count, i) for i in range(count)])  21.3 us
    reshape x1, local copies, waits for them, and re-layouts, body(): box_stack = nearby.reshape(9 * per_device, box_len, box_len, box_len)  13.8 us
    ppermute x2, waiting for transfers between devices, extended(): lax.ppermute(tail, axis, [(i, (i + 1) % count) for i in range(count)])  12.8 us
    slice x1, local copies, waits for them, and re-layouts, send_back(): collected[2]  12.1 us
  transfers between devices with their start and end apart: 8, of which 7 were waited for; matrix products, arithmetic and copies ran while one was open for 1% of the time, Pallas kernels for 0%

commit v1 on v0

v1 whole, which is shorter than its diff:
```python
import math

import jax
import jax.numpy as jnp
import numpy as np
from jax import lax
from jax.experimental import pallas as pl
from jax.experimental.pallas import tpu as pltpu
from jax.sharding import PartitionSpec as P

MESH = pl.DeviceIdType.MESH
F32 = jnp.float32
BF16 = jnp.bfloat16
BOX = 64
LANES = 128
CHUNKS = BOX * BOX // LANES
PAD = 17
ROWS = CHUNKS * BOX
EDGES = 4


def tables():
    cells = np.arange(BOX, dtype=np.float64) + 1
    sine = np.sin(math.pi * cells[:, None] * cells[None, :] / (BOX + 1))
    high = sine.astype(BF16)
    low = (sine - high.astype(np.float64)).astype(BF16)
    none = np.zeros_like(high)
    both = lambda part: np.block([[part, none], [none, part]])
    left = np.concatenate([high, high, low], axis=1)
    right = np.block([[both(high), both(low)], [both(high), both(none)]])
    eigen = 2 - 2 * np.cos(math.pi * cells / (BOX + 1))
    half = np.arange(BOX // 2)[:, None, None]
    middle = np.arange(BOX)[None, :, None]
    lane = np.arange(LANES)[None, None, :]
    total = eigen[lane // BOX * (BOX // 2) + half] + eigen[middle] + eigen[lane % BOX]
    weight = (2 / (BOX + 1)) ** 3 / total
    return left, right, weight.reshape(ROWS, LANES).astype(np.float32)


def split(values):
    high = values.astype(BF16)
    return high, (values - high.astype(F32)).astype(BF16)


def shift_matrix(amount, offset):
    row = lax.broadcasted_iota(jnp.int32, (2 * LANES, LANES), 0)
    col = lax.broadcasted_iota(jnp.int32, (2 * LANES, LANES), 1)
    cell = (col & (BOX - 1)) - offset
    inside = (row == col + amount) & (cell >= 0) & (cell < BOX)
    return jnp.where(inside, 1.0, 0.0).astype(BF16)


def rows_dot(left, values):
    high, low = split(values)
    return jnp.dot(left, jnp.concatenate([high, low, high], axis=0), preferred_element_type=F32)


def lanes_dot(values, right):
    high, low = split(values)
    both = jnp.dot(jnp.concatenate([high, low], axis=1), right, preferred_element_type=F32)
    return both[:, :LANES] + both[:, LANES:]


def beside(chunks):
    before = chunks[:-1].reshape(ROWS, LANES)
    return jnp.concatenate([before, chunks[1:].reshape(ROWS, LANES)], axis=1)


def kernel(
    orb_ref, tab_ref, left_ref, right_ref, weight_ref, out_ref,
    own, near, near_tab, tab_here, tab_near,
    padded, shifted, partner, first, first_term, field, total,
    coded, scales, got, got_scales,
    box_send, box_recv, tab_send, tab_recv, term_send, term_recv, scale_send, scale_recv, local_sem,
):
    span_x, span_y = lax.axis_size("gx"), lax.axis_size("gy")
    here_x, here_y = lax.axis_index("gx"), lax.axis_index("gy")
    sign = 1 - 2 * lax.rem(here_y, 2)

    def at(step_x, step_y):
        return (lax.rem(here_x + step_x + span_x, span_x), lax.rem(here_y + step_y + span_y, span_y))

    targets = [at(0, 1), at(sign, 0), at(1, 1), at(-1, 1)]
    users = [at(0, -1), at(-sign, 0), at(-1, -1), at(1, -1)]

    def pick(options, edge):
        chosen = options[0]
        for number in range(1, EDGES):
            chosen = tuple(jnp.where(edge == number, new, old) for new, old in zip(options[number], chosen))
        return chosen

    barrier = pltpu.get_barrier_semaphore()
    for device in targets + users:
        pl.semaphore_signal(barrier, inc=1, device_id=device, device_id_type=MESH)
    for chunk in range(CHUNKS):
        own[chunk] = orb_ref[:, chunk * LANES:(chunk + 1) * LANES]
    pl.semaphore_wait(barrier, 2 * EDGES)

    def tab_copy(edge, device):
        return pltpu.make_async_remote_copy(
            src_ref=tab_ref, dst_ref=near_tab.at[edge], send_sem=tab_send.at[edge],
            recv_sem=tab_recv.at[edge], device_id=device, device_id_type=MESH)

    def box_copy(edge, device):
        return pltpu.make_async_remote_copy(
            src_ref=own, dst_ref=near.at[edge], send_sem=box_send.at[edge],
            recv_sem=box_recv.at[edge], device_id=device, device_id_type=MESH)

    def term_copy(edge, device):
        return pltpu.make_async_remote_copy(
            src_ref=coded.at[edge], dst_ref=got.at[edge], send_sem=term_send.at[edge],
            recv_sem=term_recv.at[edge], device_id=device, device_id_type=MESH)

    def scale_copy(edge, device):
        return pltpu.make_async_remote_copy(
            src_ref=scales.at[edge], dst_ref=got_scales.at[edge], send_sem=scale_send.at[edge],
            recv_sem=scale_recv.at[edge], device_id=device, device_id_type=MESH)

    for edge in range(EDGES):
        tab_copy(edge, users[edge]).start()
        box_copy(edge, users[edge]).start()

    local = pltpu.make_async_copy(tab_ref, tab_here, local_sem)
    local.start()
    padded[...] = jnp.zeros_like(padded)
    shifted[...] = jnp.zeros_like(shifted)
    total[...] = jnp.zeros_like(total)
    local.wait()

    left = left_ref[...]
    low = lax.broadcasted_iota(jnp.int32, (BOX // 2, LANES), 1) < BOX
    me = here_x * span_y + here_y

    def pair(edge, carry):
        target = pick(targets, edge)
        other = target[0] * span_y + target[1]
        tab_copy(edge, target).wait_recv()
        copy = pltpu.make_async_copy(near_tab.at[edge], tab_near, local_sem)
        copy.start()
        copy.wait()
        listed = jnp.int32(0)
        wanted = jnp.int32(0)
        offset = [jnp.int32(0)] * 3
        for row in range(EDGES):
            mine = (tab_here[row, 0] == me) & (tab_here[row, 1] == other)
            theirs = (tab_near[row, 0] == other) & (tab_near[row, 1] == me)
            listed = jnp.where(mine, 1, listed)
            wanted = jnp.where(theirs, 1, wanted)
            for dim in range(3):
                value = jnp.where(theirs, tab_near[row, 2 + dim], offset[dim])
                offset[dim] = jnp.where(mine, tab_here[row, 2 + dim], value)
        is_mine = listed == 1
        is_live = (listed + wanted) > 0
        box_copy(edge, target).wait_recv()

        ours = own[...].astype(F32)
        theirs = near[edge].astype(F32)
        chosen = jnp.where(is_mine, ours, theirs)
        first[...] = jnp.where(is_live, chosen, 0.0).astype(BF16)
        padded[PAD:PAD + CHUNKS, BOX // 2:BOX // 2 + BOX, :] = jnp.where(is_mine, theirs, ours)

        back = -(BOX * offset[1] + offset[2])
        matrix = shift_matrix(back & (LANES - 1), offset[2])
        window = padded[pl.ds(PAD + (back >> 7), CHUNKS + 1), pl.ds(BOX // 2 - offset[0], BOX), :].astype(BF16)
        moved = jnp.dot(beside(window), matrix, preferred_element_type=F32)
        partner[...] = moved.astype(BF16).reshape(CHUNKS, BOX, LANES)
        density = moved * first[...].reshape(ROWS, LANES).astype(F32)
        along = lanes_dot(density, right_ref[...])
        for chunk in range(0, CHUNKS, 2):
            start = chunk * BOX
            wide = jnp.concatenate([along[start:start + BOX], along[start + BOX:start + 2 * BOX]], axis=1)
            wide = rows_dot(left, wide)
            for part in range(2):
                upper = wide[:BOX // 2, part * LANES:(part + 1) * LANES]
                lower = wide[BOX // 2:, part * LANES:(part + 1) * LANES]
                place = 2 * (chunk + part)
                field[pl.ds(place, BOX // 2, stride=BOX), :] = jnp.where(low, upper, pltpu.roll(lower, BOX, 1))
                field[pl.ds(place + 1, BOX // 2, stride=BOX), :] = jnp.where(low, pltpu.roll(upper, BOX, 1), lower)

        for pos in range(0, ROWS, 2 * BOX):
            wide = jnp.concatenate([field[pos:pos + BOX, :], field[pos + BOX:pos + 2 * BOX, :]], axis=1)
            factor = jnp.concatenate([weight_ref[pos:pos + BOX, :], weight_ref[pos + BOX:pos + 2 * BOX, :]], axis=1)
            wide = rows_dot(left, rows_dot(left, wide) * factor)
            field[pos:pos + BOX, :] = wide[:, :LANES]
            field[pos + BOX:pos + 2 * BOX, :] = wide[:, LANES:]

        pieces = []
        for chunk in range(0, CHUNKS, 2):
            parts = []
            for part in range(2):
                place = 2 * (chunk + part)
                even = field[pl.ds(place, BOX // 2, stride=BOX), :]
                odd = field[pl.ds(place + 1, BOX // 2, stride=BOX), :]
                upper = jnp.where(low, even, pltpu.roll(odd, BOX, 1))
                lower = jnp.where(low, pltpu.roll(even, BOX, 1), odd)
                parts.append(jnp.concatenate([upper, lower], axis=0))
            wide = rows_dot(left, jnp.concatenate(parts, axis=1))
            pieces += [wide[:, :LANES], wide[:, LANES:]]
        potential = lanes_dot(jnp.concatenate(pieces, axis=0), right_ref[...])
        potential = -potential.reshape(CHUNKS, BOX, LANES)
        first_term[...] = potential * partner[...].astype(F32)
        shifted[PAD:PAD + CHUNKS, BOX // 2:BOX // 2 + BOX, :] = potential * first[...].astype(F32)

        ahead = BOX * offset[1] + offset[2]
        matrix = shift_matrix(ahead & (LANES - 1), -offset[2])
        window = shifted[pl.ds(PAD + (ahead >> 7), CHUNKS + 1), pl.ds(BOX // 2 + offset[0], BOX), :]
        high, rest = split(window)
        second_term = jnp.dot(beside(high), matrix, preferred_element_type=F32)
        second_term += jnp.dot(beside(rest), matrix, preferred_element_type=F32)
        second_term = second_term.reshape(CHUNKS, BOX, LANES)
        one = first_term[...]
        total[...] += jnp.where(is_mine, one, second_term)
        sent = jnp.where(is_mine, second_term, one)
        largest = jnp.max(jnp.abs(sent), axis=1, keepdims=True)
        safe = largest > 1e-33
        factor = jnp.where(safe, 32767.0 / jnp.where(safe, largest, 1.0), 0.0)
        coded[edge] = jnp.round(sent * factor).astype(jnp.int32).astype(jnp.int16)
        scales[edge] = (largest * (1.0 / 32767.0)).reshape(CHUNKS, LANES)
        scale_copy(edge, target).start()
        term_copy(edge, target).start()
        return carry

    lax.fori_loop(0, EDGES, pair, 0)

    for edge in range(EDGES):
        scale_copy(edge, users[edge]).wait_recv()
        term_copy(edge, users[edge]).wait_recv()
    for chunk in range(CHUNKS):
        value = total[chunk]
        for edge in range(EDGES):
            value += got[edge, chunk].astype(F32) * got_scales[edge, chunk:chunk + 1, :]
        out_ref[:, chunk * LANES:(chunk + 1) * LANES] = value
    for edge in range(EDGES):
        tab_copy(edge, users[edge]).wait_send()
        box_copy(edge, users[edge]).wait_send()
        scale_copy(edge, targets[edge]).wait_send()
        term_copy(edge, targets[edge]).wait_send()


def body(orbitals, pair_table):
    left, right, weight = tables()
    table = jnp.pad(pair_table.reshape(EDGES, 5), ((0, 4), (0, LANES - 5)), constant_values=-1)
    vmem = pl.BlockSpec(memory_space=pltpu.VMEM)
    cube = (CHUNKS, BOX, LANES)
    wide = (CHUNKS + 2 * PAD, 2 * BOX, LANES)
    dma = pltpu.SemaphoreType.DMA((EDGES,))
    result = pl.pallas_call(
        kernel,
        out_shape=jax.ShapeDtypeStruct((BOX, BOX * BOX), F32),
        in_specs=[vmem] * 5,
        out_specs=vmem,
        scratch_shapes=[
            pltpu.VMEM(cube, BF16),
            pltpu.VMEM((EDGES,) + cube, BF16),
            pltpu.VMEM((EDGES, 8, LANES), jnp.int32),
            pltpu.SMEM((8, LANES), jnp.int32),
            pltpu.SMEM((8, LANES), jnp.int32),
            pltpu.VMEM(wide, F32),
            pltpu.VMEM(wide, F32),
            pltpu.VMEM(cube, BF16),
            pltpu.VMEM(cube, BF16),
            pltpu.VMEM(cube, F32),
            pltpu.VMEM((ROWS, LANES), F32),
            pltpu.VMEM(cube, F32),
            pltpu.VMEM((EDGES,) + cube, jnp.int16),
            pltpu.VMEM((EDGES, CHUNKS, LANES), F32),
            pltpu.VMEM((EDGES,) + cube, jnp.int16),
            pltpu.VMEM((EDGES, CHUNKS, LANES), F32),
            dma, dma, dma, dma, dma, dma, dma, dma,
            pltpu.SemaphoreType.DMA,
        ],
        compiler_params=pltpu.CompilerParams(
            collective_id=0, has_side_effects=True, vmem_limit_bytes=56 * 1024 * 1024),
    )(orbitals.reshape(BOX, BOX * BOX), table, jnp.asarray(left), jnp.asarray(right), jnp.asarray(weight))
    return result.reshape(orbitals.shape)


def solution(mesh):
    in_specs = (P("gx", "gy", None, None, None), P("gx", "gy", None, None))
    out_specs = P("gx", "gy", None, None, None)
    return jax.shard_map(body, mesh=mesh, in_specs=in_specs, out_specs=out_specs, check_vma=False)
```

time: 446 us -> 72.2 us (0.16)
  the two profiles are of different devices: /device:TPU:26 before, /device:TPU:6 now
where the time goes in v1:
time: 72.2 us; the launch traced here: 72 us
  Pallas kernels  68.4 us (95%)
  local copies, waits for them, and re-layouts  3.55 us (5%)
    pallas_call x1, Pallas kernels, body(): pl.pallas_call(kernel, out_shape=jax.ShapeDtypeStruct((BOX, BOX * BOX), F...  68.4 us
    unnamed x3, local copies, waits for them, and re-layouts  2.95 us

profile of v1, /device:TPU:6, one launch (start us, length us, event | category | flops | bytes accessed | tf_op | source)
XLA Modules:
  0.0 72.0 jit_solution(7077889400627580906)
XLA Ops:
  0.0 0.0 copy-start
  0.0 0.7 copy-done
  0.7 0.6 pad.4.tab_ref
  1.3 68.4 %shard_map.55 = f32[64,4096]{1,0:T(8,128)} custom-call(bf16[64,4096]{1,0:T(8,128)(2,1)} %bitcast.4, s32[8,128]{1,0:T(8,128)} %pad.4.tab_ref, bf16[64,192]{1,0:T(8,128)(2,1)} %constant.8.clone.left_ref, bf16[256,256]{1,0:T(8,128)(2,1)} %constant.9.clone.right_ref, f32[2048,128]{1,0:T(8,128)} %constant.10.clone.weight_ref), custom_call_target="tpu_custom_call" | custom-call | tf_op jit(solution)/shard_map/pallas_call | solution.py:247
  69.7 2.3 %copy.7 = f32[1,1,1,64,4096]{4,3,2,1,0:T(8,128)} copy(f32[1,1,1,64,4096]{4,3,2,1,0:T(8,128)} %bitcast.3) | data formatting | bytes 2097152
Async XLA Ops:
  0.0 0.7 copy-start

commit v2 on v1

--- a/solution.py
+++ b/solution.py
@@ -75,13 +75,17 @@
 ):
     span_x, span_y = lax.axis_size("gx"), lax.axis_size("gy")
     here_x, here_y = lax.axis_index("gx"), lax.axis_index("gy")
-    sign = 1 - 2 * lax.rem(here_y, 2)
+    core = lax.rem(here_y, 2)
 
     def at(step_x, step_y):
         return (lax.rem(here_x + step_x + span_x, span_x), lax.rem(here_y + step_y + span_y, span_y))
 
-    targets = [at(0, 1), at(sign, 0), at(1, 1), at(-1, 1)]
-    users = [at(0, -1), at(-sign, 0), at(-1, -1), at(1, -1)]
+    def by_core(on_first, on_second):
+        return at(*(jnp.where(core == 0, one, two) for one, two in zip(on_first, on_second)))
+
+    targets = [by_core((1, 0), (0, -1)), by_core((0, -1), (-1, 0)), by_core((1, -1), (-1, -1)), by_core((-1, -1), (1, -1))]
+    users = [at(0, 1), by_core((-1, 0), (1, 0)), by_core((1, 1), (-1, 1)), by_core((-1, 1), (1, 1))]
+    box_slots = [core, core, 2, 3]
 
     def pick(options, edge):
         chosen = options[0]
@@ -90,35 +94,42 @@
         return chosen
 
     barrier = pltpu.get_barrier_semaphore()
-    for device in targets + users:
-        pl.semaphore_signal(barrier, inc=1, device_id=device, device_id_type=MESH)
+    for step_x, step_y in ((1, 0), (-1, 0), (0, -1), (1, -1), (-1, -1)):
+        pl.semaphore_signal(barrier, inc=1, device_id=at(step_x, step_y), device_id_type=MESH)
+
+    @pl.when(here_y < span_y - 1)
+    def _():
+        for step_x in (0, 1, -1):
+            pl.semaphore_signal(barrier, inc=1, device_id=at(step_x, 1), device_id_type=MESH)
+
     for chunk in range(CHUNKS):
         own[chunk] = orb_ref[:, chunk * LANES:(chunk + 1) * LANES]
-    pl.semaphore_wait(barrier, 2 * EDGES)
-
-    def tab_copy(edge, device):
+    pl.semaphore_wait(barrier, jnp.where(here_y == 0, 5, 8))
+
+    def tab_copy(edge, slot, device):
         return pltpu.make_async_remote_copy(
-            src_ref=tab_ref, dst_ref=near_tab.at[edge], send_sem=tab_send.at[edge],
-            recv_sem=tab_recv.at[edge], device_id=device, device_id_type=MESH)
-
-    def box_copy(edge, device):
+            src_ref=tab_ref, dst_ref=near_tab.at[slot], send_sem=tab_send.at[edge],
+            recv_sem=tab_recv.at[slot], device_id=device, device_id_type=MESH)
+
+    def box_copy(edge, slot, device):
         return pltpu.make_async_remote_copy(
-            src_ref=own, dst_ref=near.at[edge], send_sem=box_send.at[edge],
-            recv_sem=box_recv.at[edge], device_id=device, device_id_type=MESH)
-
-    def term_copy(edge, device):
+            src_ref=own, dst_ref=near.at[slot], send_sem=box_send.at[edge],
+            recv_sem=box_recv.at[slot], device_id=device, device_id_type=MESH)
+
+    def term_copy(edge, slot, device):
         return pltpu.make_async_remote_copy(
-            src_ref=coded.at[edge], dst_ref=got.at[edge], send_sem=term_send.at[edge],
-            recv_sem=term_recv.at[edge], device_id=device, device_id_type=MESH)
-
-    def scale_copy(edge, device):
+            src_ref=coded.at[edge], dst_ref=got.at[slot], send_sem=term_send.at[edge],
+            recv_sem=term_recv.at[slot], device_id=device, device_id_type=MESH)
+
+    def scale_copy(edge, slot, device):
         return pltpu.make_async_remote_copy(
-            src_ref=scales.at[edge], dst_ref=got_scales.at[edge], send_sem=scale_send.at[edge],
-            recv_sem=scale_recv.at[edge], device_id=device, device_id_type=MESH)
+            src_ref=scales.at[edge], dst_ref=got_scales.at[slot], send_sem=scale_send.at[edge],
+            recv_sem=scale_recv.at[slot], device_id=device, device_id_type=MESH)
 
     for edge in range(EDGES):
-        tab_copy(edge, users[edge]).start()
-        box_copy(edge, users[edge]).start()
+        tab_copy(edge, box_slots[edge], users[edge]).start()
+    for edge in range(2):
+        box_copy(edge, box_slots[edge], users[edge]).start()
 
     local = pltpu.make_async_copy(tab_ref, tab_here, local_sem)
     local.start()
@@ -134,7 +145,7 @@
     def pair(edge, carry):
         target = pick(targets, edge)
         other = target[0] * span_y + target[1]
-        tab_copy(edge, target).wait_recv()
+        tab_copy(edge, edge, target).wait_recv()
         copy = pltpu.make_async_copy(near_tab.at[edge], tab_near, local_sem)
         copy.start()
         copy.wait()
@@ -151,7 +162,15 @@
                 offset[dim] = jnp.where(mine, tab_here[row, 2 + dim], value)
         is_mine = listed == 1
         is_live = (listed + wanted) > 0
-        box_copy(edge, target).wait_recv()
+        box_copy(edge, edge, target).wait_recv()
+
+        @pl.when(edge == core)
+        def _():
+            box_copy(2, box_slots[2], users[2]).start()
+
+        @pl.when(edge == core + 1)
+        def _():
+            box_copy(3, box_slots[3], users[3]).start()
 
         ours = own[...].astype(F32)
         theirs = near[edge].astype(F32)
@@ -216,30 +235,31 @@
         factor = jnp.where(safe, 32767.0 / jnp.where(safe, largest, 1.0), 0.0)
         coded[edge] = jnp.round(sent * factor).astype(jnp.int32).astype(jnp.int16)
         scales[edge] = (largest * (1.0 / 32767.0)).reshape(CHUNKS, LANES)
-        scale_copy(edge, target).start()
-        term_copy(edge, target).start()
+        term_slot = jnp.where(edge < 2, lax.rem(edge + 1 - core, 2), edge)
+        scale_copy(edge, term_slot, target).start()
+        term_copy(edge, term_slot, target).start()
         return carry
 
     lax.fori_loop(0, EDGES, pair, 0)
 
     for edge in range(EDGES):
-        scale_copy(edge, users[edge]).wait_recv()
-        term_copy(edge, users[edge]).wait_recv()
+        scale_copy(edge, edge, users[edge]).wait_recv()
+        term_copy(edge, edge, users[edge]).wait_recv()
     for chunk in range(CHUNKS):
         value = total[chunk]
         for edge in range(EDGES):
             value += got[edge, chunk].astype(F32) * got_scales[edge, chunk:chunk + 1, :]
         out_ref[:, chunk * LANES:(chunk + 1) * LANES] = value
     for edge in range(EDGES):
-        tab_copy(edge, users[edge]).wait_send()
-        box_copy(edge, users[edge]).wait_send()
-        scale_copy(edge, targets[edge]).wait_send()
-        term_copy(edge, targets[edge]).wait_send()
+        tab_copy(edge, edge, users[edge]).wait_send()
+        box_copy(edge, edge, users[edge]).wait_send()
+        scale_copy(edge, edge, targets[edge]).wait_send()
+        term_copy(edge, edge, targets[edge]).wait_send()
 
 
 def body(orbitals, pair_table):
     left, right, weight = tables()
-    table = jnp.pad(pair_table.reshape(EDGES, 5), ((0, 4), (0, LANES - 5)), constant_values=-1)
+    table = pair_table.reshape(EDGES, 5)
     vmem = pl.BlockSpec(memory_space=pltpu.VMEM)
     cube = (CHUNKS, BOX, LANES)
     wide = (CHUNKS + 2 * PAD, 2 * BOX, LANES)
@@ -252,9 +272,9 @@
         scratch_shapes=[
             pltpu.VMEM(cube, BF16),
             pltpu.VMEM((EDGES,) + cube, BF16),
-            pltpu.VMEM((EDGES, 8, LANES), jnp.int32),
-            pltpu.SMEM((8, LANES), jnp.int32),
-            pltpu.SMEM((8, LANES), jnp.int32),
+            pltpu.VMEM((EDGES, EDGES, 5), jnp.int32),
+            pltpu.SMEM((EDGES, 5), jnp.int32),
+            pltpu.SMEM((EDGES, 5), jnp.int32),
             pltpu.VMEM(wide, F32),
             pltpu.VMEM(wide, F32),
             pltpu.VMEM(cube, BF16),

time: 72.2 us -> 62 us (0.86)
  the two profiles are of different devices: /device:TPU:6 before, /device:TPU:193 now
where the time goes in v2:
time: 62 us; the launch traced here: 61.8 us
  Pallas kernels  59.6 us (96%)
  local copies, waits for them, and re-layouts  2.27 us (4%)
    pallas_call x1, Pallas kernels, body(): pl.pallas_call(kernel, out_shape=jax.ShapeDtypeStruct((BOX, BOX * BOX), F...  59.6 us
    unnamed x1, local copies, waits for them, and re-layouts  2.27 us

profile of v2, /device:TPU:193, one launch (start us, length us, event | category | flops | bytes accessed | tf_op | source)
XLA Modules:
  0.0 61.8 jit_solution(14586055077536102730)
XLA Ops:
  0.0 59.6 %shard_map.55 = f32[64,4096]{1,0:T(8,128)} custom-call(bf16[64,4096]{1,0:T(8,128)(2,1)} %bitcast.4, s32[4,5]{1,0:T(4,128)} %bitcast.5, bf16[64,192]{1,0:T(8,128)(2,1)} %constant.6.clone.left_ref, bf16[256,256]{1,0:T(8,128)(2,1)} %constant.7.clone.right_ref, f32[2048,128]{1,0:T(8,128)} %constant.8.clone.weight_ref), custom_call_target="tpu_custom_call" | custom-call | tf_op jit(solution)/shard_map/pallas_call | solution.py:267
  59.6 2.3 %copy.7 = f32[1,1,1,64,4096]{4,3,2,1,0:T(8,128)} copy(f32[1,1,1,64,4096]{4,3,2,1,0:T(8,128)} %bitcast.3) | data formatting | bytes 2097152

commit v3 on v0

v3 whole, which is shorter than its diff:
```python
import math

import jax
import jax.numpy as jnp
import numpy as np
from jax import lax
from jax.experimental import pallas as pl
from jax.experimental.pallas import tpu as pltpu
from jax.sharding import PartitionSpec as P

MESH = pl.DeviceIdType.MESH
F32 = jnp.float32
BF16 = jnp.bfloat16
BOX = 64
HALF = BOX // 2
LANES = 128
CHUNKS = BOX * BOX // LANES
PAD = 17
ROWS = 4
NEAR = 8
GROUP = 16


def tables():
    cells = np.arange(BOX, dtype=np.float64) + 1
    sine = np.sin(math.pi * cells[:, None] * cells[None, :] / (BOX + 1))
    high = sine.astype(BF16)
    low = (sine - high.astype(np.float64)).astype(BF16)
    none = np.zeros_like(high)
    both = lambda part: np.block([[part, none], [none, part]])
    left = np.concatenate([high, high, low], axis=1)
    right = np.block([[both(high), both(low)], [both(high), both(none)]])
    eigen = 2 - 2 * np.cos(math.pi * cells / (BOX + 1))
    row = np.arange(HALF)[:, None]
    lane = np.arange(LANES)[None, :]
    middle = 2 + eigen[lane // BOX * HALF + row] + eigen[lane % BOX]
    ratios = [1 / middle]
    for _ in range(HALF - 1):
        ratios.append(1 / (middle - ratios[-1]))
    ratios.append(1 / (1 - ratios[-1] ** 2))
    return left, right, np.stack(ratios).astype(np.float32)


def split(values):
    high = values.astype(BF16)
    return high, (values - high.astype(F32)).astype(BF16)


def rows_dot(left, values):
    high, low = split(values)
    return jnp.dot(left, jnp.concatenate([high, low, high], axis=0), preferred_element_type=F32)


def lanes_dot(values, right):
    high, low = split(values)
    both = jnp.dot(jnp.concatenate([high, low], axis=1), right, preferred_element_type=F32)
    return both[:, :LANES] + both[:, LANES:]


def shift_masks(amount, offset):
    lane = lax.broadcasted_iota(jnp.int32, (BOX, LANES), 1)
    cell = (lane & (BOX - 1)) - offset
    inside = (cell >= 0) & (cell < BOX)
    return (lane < LANES - amount) & inside, (lane >= LANES - amount) & inside


def shifted(source, slot, chunks, row, flat, offset):
    start, amount = PAD + (flat >> 7), flat & (LANES - 1)
    here, after = shift_masks(amount, offset)
    turned = {}

    def turn(chunk):
        if chunk not in turned:
            values = source[slot, start + chunk, pl.ds(row, BOX), :]
            turned[chunk] = pltpu.roll(values, LANES - amount, 1)
        return turned[chunk]

    return {chunk: jnp.where(here, turn(chunk), jnp.where(after, turn(chunk + 1), 0.0)) for chunk in chunks}


def kernel(
    orb_ref, tab_ref, left_ref, right_ref, ratio_ref, out_ref,
    own, near, tab_here, tab_near, padded, partner, field,
    box_send, box_recv, tab_send, tab_recv, ready, local_sem,
):
    span_x, span_y = lax.axis_size("gx"), lax.axis_size("gy")
    here_x, here_y = lax.axis_index("gx"), lax.axis_index("gy")
    core = lax.rem(here_y, 2)
    sign = 1 - 2 * core

    def at(step_x, step_y):
        return (lax.rem(here_x + step_x + span_x, span_x), lax.rem(here_y + step_y + span_y, span_y))

    twin, beyond, ahead, behind = at(0, sign), at(0, -sign), at(1, 0), at(-1, 0)
    owners = [twin, beyond, ahead, behind, at(1, sign), at(-1, sign), at(1, -sign), at(-1, -sign)]
    dests = [twin, beyond, behind, ahead, twin, twin, beyond, beyond]

    def by_step(step, order):
        slot = order[0]
        for number in range(1, NEAR):
            slot = jnp.where(step == number, order[number], slot)
        return slot

    def pick(slot):
        chosen = owners[0]
        for number in range(1, NEAR):
            chosen = tuple(jnp.where(slot == number, new, old) for new, old in zip(owners[number], chosen))
        return chosen

    asks = jnp.where(core == 0, here_y == 0, here_y < span_y - 1)
    barrier = pltpu.get_barrier_semaphore()
    for device in (twin, ahead, behind):
        pl.semaphore_signal(barrier, inc=1, device_id=device, device_id_type=MESH)

    @pl.when(asks)
    def _():
        pl.semaphore_signal(barrier, inc=1, device_id=beyond, device_id_type=MESH)

    for chunk in range(CHUNKS):
        own[chunk] = orb_ref[:, chunk * LANES:(chunk + 1) * LANES]
    pl.semaphore_wait(barrier, jnp.where(asks, 3, 4))

    def box_copy(slot, source):
        return pltpu.make_async_remote_copy(
            src_ref=source, dst_ref=near.at[slot], send_sem=box_send.at[slot],
            recv_sem=box_recv.at[slot], device_id=dests[slot] if isinstance(slot, int) else twin, device_id_type=MESH)

    def tab_copy(slot, source):
        return pltpu.make_async_remote_copy(
            src_ref=source, dst_ref=tab_near.at[slot], send_sem=tab_send.at[slot],
            recv_sem=tab_recv.at[slot], device_id=dests[slot] if isinstance(slot, int) else twin, device_id_type=MESH)

    def send_own(slot):
        tab_copy(slot, tab_here).start()
        box_copy(slot, own).start()

    def hand_on(slot, source):
        tab_copy(slot, tab_near.at[source]).start()
        box_copy(slot, near.at[source]).start()

    local = pltpu.make_async_copy(tab_ref, tab_here, local_sem)
    local.start()
    local.wait()

    @pl.when(jnp.logical_not(asks))
    def _():
        pl.semaphore_signal(ready, inc=1, device_id=beyond, device_id_type=MESH)

    @pl.when(core == 0)
    def _():
        send_own(3)

    @pl.when(core == 1)
    def _():
        send_own(2)

    send_own(0)

    @pl.when(jnp.logical_not(asks))
    def _():
        send_own(1)

    padded[...] = jnp.zeros_like(padded)
    out_ref[...] = jnp.zeros_like(out_ref)
    padded[0, PAD:PAD + CHUNKS, HALF:HALF + BOX, :] = own[...].astype(F32)

    @pl.when(asks & (core == 1))
    def _():
        pl.semaphore_wait(ready, 1)
        send_own(1)

    left, right = left_ref[...], right_ref[...]
    low = lax.broadcasted_iota(jnp.int32, (HALF, LANES), 1) < BOX
    me = here_x * span_y + here_y

    def pair(step, carry):
        on_first = jnp.where(here_y == 0, by_step(step, (0, 3, 4, 2, 5, 1, 6, 7)), by_step(step, (0, 3, 1, 2, 4, 5, 6, 7)))
        slot = jnp.where(core == 0, on_first, by_step(step, (0, 2, 5, 3, 1, 4, 7, 6)))
        owner = pick(slot)
        other = owner[0] * span_y + owner[1]

        @pl.when((step == 1) & (core == 0))
        def _():
            box_copy(3, own).wait_send()
            send_own(2)

        @pl.when((step == 1) & (core == 1))
        def _():
            box_copy(2, own).wait_send()
            send_own(3)

        @pl.when((step == 1) & (here_y == 0))
        def _():
            pl.semaphore_wait(ready, 1)
            send_own(1)

        tab_copy(slot, tab_here).wait_recv()
        box_copy(slot, own).wait_recv()

        @pl.when(slot == 2)
        def _():
            hand_on(6, 2)
            hand_on(4, 2)

        @pl.when(slot == 3)
        def _():
            hand_on(7, 3)
            hand_on(5, 3)

        listed = jnp.int32(0)
        wanted = jnp.int32(0)
        offset = [jnp.int32(0)] * 3
        for row in range(ROWS):
            mine = (tab_here[row, 0] == me) & (tab_here[row, 1] == other)
            theirs = (tab_near[slot, row, 0] == other) & (tab_near[slot, row, 1] == me)
            listed = jnp.where(mine, 1, listed)
            wanted = jnp.where(theirs, 1, wanted)
            for dim in range(3):
                value = jnp.where(theirs, tab_near[slot, row, 2 + dim], offset[dim])
                offset[dim] = jnp.where(mine, tab_here[row, 2 + dim], value)
        is_mine = listed == 1
        scale = jnp.where(listed + wanted > 0, -((2 / (BOX + 1)) ** 2), 0.0)
        second = listed
        first = 1 - listed
        padded[1, PAD:PAD + CHUNKS, HALF:HALF + BOX, :] = near[slot].astype(F32)

        flat = -(BOX * offset[1] + offset[2])
        order = [chunk for number in range(CHUNKS // 2) for chunk in (number, CHUNKS - 1 - number)]
        front = back = None
        for place in range(0, CHUNKS, GROUP):
            chunks = order[place:place + GROUP]
            moved = shifted(padded, second, sorted(chunks), HALF - offset[0], flat, offset[2])
            products = []
            for chunk in chunks:
                fixed = padded[first, PAD + chunk, HALF:HALF + BOX, :]
                products.append(moved[chunk] * fixed)
                partner[chunk] = jnp.where(is_mine, moved[chunk], fixed).astype(BF16)
            along = lanes_dot(jnp.concatenate(products, axis=0), right)
            for number in range(0, GROUP, 2):
                begin = number * BOX
                wide = jnp.concatenate([along[begin:begin + BOX], along[begin + BOX:begin + 2 * BOX]], axis=1)
                wide = rows_dot(left, wide)
                layers = []
                for part in range(2):
                    upper = wide[:HALF, part * LANES:(part + 1) * LANES]
                    lower = wide[HALF:, part * LANES:(part + 1) * LANES]
                    layers.append(jnp.where(low, upper, pltpu.roll(lower, BOX, 1)))
                    layers.append(jnp.where(low, pltpu.roll(upper, BOX, 1), lower))
                for layer, one, two in ((0, layers[0], layers[3]), (1, layers[1], layers[2])):
                    layer += 2 * chunks[number]
                    if layer > 0:
                        one, two = one + front, two + back
                    front, back = one * ratio_ref[layer], two * ratio_ref[layer]
                    field[layer] = front
                    field[BOX - 1 - layer] = back

        last, closing = ratio_ref[HALF - 1], ratio_ref[HALF]
        solved = {HALF - 1: (front + last * back) * closing, HALF: (back + last * front) * closing}
        order = [chunk for number in reversed(range(CHUNKS // 2)) for chunk in (number, CHUNKS - 1 - number)]
        for place in range(0, CHUNKS, GROUP):
            chunks = order[place:place + GROUP]
            pieces = []
            for number in range(0, GROUP, 2):
                for layer in (2 * chunks[number] + 1, 2 * chunks[number]):
                    if layer < HALF - 1:
                        mirror = BOX - 1 - layer
                        solved[layer] = field[layer] + ratio_ref[layer] * solved[layer + 1]
                        solved[mirror] = field[mirror] + ratio_ref[layer] * solved[mirror - 1]
                parts = []
                for chunk in chunks[number:number + 2]:
                    even, odd = solved[2 * chunk], solved[2 * chunk + 1]
                    upper = jnp.where(low, even, pltpu.roll(odd, BOX, 1))
                    lower = jnp.where(low, pltpu.roll(even, BOX, 1), odd)
                    parts.append(jnp.concatenate([upper, lower], axis=0))
                wide = rows_dot(left, jnp.concatenate(parts, axis=1))
                pieces += [wide[:, :LANES], wide[:, LANES:]]
            potential = lanes_dot(jnp.concatenate(pieces, axis=0), right)
            for number, chunk in enumerate(chunks):
                values = potential[number * BOX:(number + 1) * BOX] * scale
                padded[2, PAD + chunk, HALF:HALF + BOX, :] = values * partner[chunk].astype(F32)

        offset = [jnp.where(is_mine, 0, value) for value in offset]
        flat = BOX * offset[1] + offset[2]
        for place in range(0, CHUNKS, GROUP):
            moved = shifted(padded, 2, range(place, place + GROUP), HALF + offset[0], flat, -offset[2])
            for chunk in range(place, place + GROUP):
                out_ref[:, chunk * LANES:(chunk + 1) * LANES] += moved[chunk]
        return carry

    lax.fori_loop(0, NEAR, pair, 0)

    for slot in range(NEAR):
        source = own if slot < 4 else near.at[2 + slot % 2]
        tab_copy(slot, tab_here).wait_send()
        if slot not in (2, 3):
            box_copy(slot, source).wait_send()

    @pl.when(core == 0)
    def _():
        box_copy(2, own).wait_send()

    @pl.when(core == 1)
    def _():
        box_copy(3, own).wait_send()


def body(orbitals, pair_table):
    left, right, ratios = tables()
    vmem = pl.BlockSpec(memory_space=pltpu.VMEM)
    cube = (CHUNKS, BOX, LANES)
    dma = pltpu.SemaphoreType.DMA((NEAR,))
    result = pl.pallas_call(
        kernel,
        out_shape=jax.ShapeDtypeStruct((BOX, BOX * BOX), F32),
        in_specs=[vmem] * 5,
        out_specs=vmem,
        scratch_shapes=[
            pltpu.VMEM(cube, BF16),
            pltpu.VMEM((NEAR,) + cube, BF16),
            pltpu.SMEM((ROWS, 5), jnp.int32),
            pltpu.SMEM((NEAR, ROWS, 5), jnp.int32),
            pltpu.VMEM((3, CHUNKS + 2 * PAD, 2 * BOX, LANES), F32),
            pltpu.VMEM(cube, BF16),
            pltpu.VMEM((BOX, HALF, LANES), F32),
            dma, dma, dma, dma,
            pltpu.SemaphoreType.REGULAR,
            pltpu.SemaphoreType.DMA,
        ],
        compiler_params=pltpu.CompilerParams(
            collective_id=0, has_side_effects=True, vmem_limit_bytes=56 * 1024 * 1024),
    )(orbitals.reshape(BOX, BOX * BOX), pair_table.reshape(ROWS, 5), jnp.asarray(left), jnp.asarray(right), jnp.asarray(ratios))
    return result.reshape(orbitals.shape)


def solution(mesh):
    in_specs = (P("gx", "gy", None, None, None), P("gx", "gy", None, None))
    out_specs = P("gx", "gy", None, None, None)
    return jax.shard_map(body, mesh=mesh, in_specs=in_specs, out_specs=out_specs, check_vma=False)
```

time: 446 us -> 44.1 us (0.10)
  the two profiles are of different devices: /device:TPU:26 before, /device:TPU:1 now
where the time goes in v3:
time: 44.1 us; the launch traced here: 43.9 us
  Pallas kernels  41.7 us (95%)
  local copies, waits for them, and re-layouts  2.27 us (5%)
    pallas_call x1, Pallas kernels, body(): pl.pallas_call(kernel, out_shape=jax.ShapeDtypeStruct((BOX, BOX * BOX), F...  41.7 us
    unnamed x1, local copies, waits for them, and re-layouts  2.27 us

profile of v3, /device:TPU:1, one launch (start us, length us, event | category | flops | bytes accessed | tf_op | source)
XLA Modules:
  0.0 43.9 jit_solution(6731055768363732709)
XLA Ops:
  0.0 41.7 %shard_map.55 = f32[64,4096]{1,0:T(8,128)} custom-call(bf16[64,4096]{1,0:T(8,128)(2,1)} %bitcast.4, s32[4,5]{1,0:T(4,128)} %bitcast.5, bf16[64,192]{1,0:T(8,128)(2,1)} %constant.6.clone.left_ref, bf16[256,256]{1,0:T(8,128)(2,1)} %constant.7.clone.right_ref, f32[33,32,128]{2,1,0:T(8,128)} %constant.8.clone.ratio_ref), custom_call_target="tpu_custom_call" | custom-call | tf_op jit(solution)/shard_map/pallas_call | solution.py:312
  41.7 2.3 %copy.7 = f32[1,1,1,64,4096]{4,3,2,1,0:T(8,128)} copy(f32[1,1,1,64,4096]{4,3,2,1,0:T(8,128)} %bitcast.3) | data formatting | bytes 2097152

commit v4 on v3

--- a/solution.py
+++ b/solution.py
@@ -79,7 +79,8 @@
 
 
 def kernel(
-    orb_ref, tab_ref, left_ref, right_ref, ratio_ref, out_ref,
+    orb_hbm, tab_hbm, left_hbm, right_hbm, ratio_hbm, out_ref,
+    orb_ref, left_ref, right_ref, ratio_ref,
     own, near, tab_here, tab_near, padded, partner, field,
     box_send, box_recv, tab_send, tab_recv, ready, local_sem,
 ):
@@ -107,18 +108,26 @@
             chosen = tuple(jnp.where(slot == number, new, old) for new, old in zip(owners[number], chosen))
         return chosen
 
-    asks = jnp.where(core == 0, here_y == 0, here_y < span_y - 1)
     barrier = pltpu.get_barrier_semaphore()
     for device in (twin, ahead, behind):
         pl.semaphore_signal(barrier, inc=1, device_id=device, device_id_type=MESH)
 
-    @pl.when(asks)
+    @pl.when(here_y < span_y - 1)
     def _():
         pl.semaphore_signal(barrier, inc=1, device_id=beyond, device_id_type=MESH)
 
+    loads = [
+        pltpu.make_async_copy(source, dest, local_sem.at[number])
+        for number, (source, dest) in enumerate((
+            (orb_hbm, orb_ref), (tab_hbm, tab_here), (left_hbm, left_ref), (right_hbm, right_ref), (ratio_hbm, ratio_ref)))
+    ]
+    for load in loads:
+        load.start()
+    loads[0].wait()
     for chunk in range(CHUNKS):
         own[chunk] = orb_ref[:, chunk * LANES:(chunk + 1) * LANES]
-    pl.semaphore_wait(barrier, jnp.where(asks, 3, 4))
+    loads[1].wait()
+    pl.semaphore_wait(barrier, jnp.where(here_y == 0, 3, 4))
 
     def box_copy(slot, source):
         return pltpu.make_async_remote_copy(
@@ -138,14 +147,14 @@
         tab_copy(slot, tab_near.at[source]).start()
         box_copy(slot, near.at[source]).start()
 
-    local = pltpu.make_async_copy(tab_ref, tab_here, local_sem)
-    local.start()
-    local.wait()
-
-    @pl.when(jnp.logical_not(asks))
+    @pl.when(here_y == span_y - 1)
     def _():
         pl.semaphore_signal(ready, inc=1, device_id=beyond, device_id_type=MESH)
 
+    @pl.when(here_y > 0)
+    def _():
+        send_own(1)
+
     @pl.when(core == 0)
     def _():
         send_own(3)
@@ -155,19 +164,11 @@
         send_own(2)
 
     send_own(0)
-
-    @pl.when(jnp.logical_not(asks))
-    def _():
-        send_own(1)
-
     padded[...] = jnp.zeros_like(padded)
     out_ref[...] = jnp.zeros_like(out_ref)
     padded[0, PAD:PAD + CHUNKS, HALF:HALF + BOX, :] = own[...].astype(F32)
-
-    @pl.when(asks & (core == 1))
-    def _():
-        pl.semaphore_wait(ready, 1)
-        send_own(1)
+    for load in loads[2:]:
+        load.wait()
 
     left, right = left_ref[...], right_ref[...]
     low = lax.broadcasted_iota(jnp.int32, (HALF, LANES), 1) < BOX
@@ -306,15 +307,20 @@
 
 def body(orbitals, pair_table):
     left, right, ratios = tables()
-    vmem = pl.BlockSpec(memory_space=pltpu.VMEM)
+    operands = [orbitals.reshape(BOX, BOX * BOX), pair_table.reshape(ROWS, 5)]
+    operands += [jnp.asarray(table) for table in (left, right, ratios)]
     cube = (CHUNKS, BOX, LANES)
     dma = pltpu.SemaphoreType.DMA((NEAR,))
     result = pl.pallas_call(
         kernel,
-        out_shape=jax.ShapeDtypeStruct((BOX, BOX * BOX), F32),
-        in_specs=[vmem] * 5,
-        out_specs=vmem,
+        out_shape=pltpu.VMEM((BOX, BOX * BOX), F32),
+        in_specs=[pl.BlockSpec(memory_space=pltpu.HBM)] * 5,
+        out_specs=pl.BlockSpec(memory_space=pltpu.VMEM),
         scratch_shapes=[
+            pltpu.VMEM((BOX, BOX * BOX), BF16),
+            pltpu.VMEM(left.shape, BF16),
+            pltpu.VMEM(right.shape, BF16),
+            pltpu.VMEM(ratios.shape, F32),
             pltpu.VMEM(cube, BF16),
             pltpu.VMEM((NEAR,) + cube, BF16),
             pltpu.SMEM((ROWS, 5), jnp.int32),
@@ -324,11 +330,11 @@
             pltpu.VMEM((BOX, HALF, LANES), F32),
             dma, dma, dma, dma,
             pltpu.SemaphoreType.REGULAR,
-            pltpu.SemaphoreType.DMA,
+            pltpu.SemaphoreType.DMA((5,)),
         ],
         compiler_params=pltpu.CompilerParams(
-            collective_id=0, has_side_effects=True, vmem_limit_bytes=56 * 1024 * 1024),
-    )(orbitals.reshape(BOX, BOX * BOX), pair_table.reshape(ROWS, 5), jnp.asarray(left), jnp.asarray(right), jnp.asarray(ratios))
+            collective_id=0, has_side_effects=True, vmem_limit_bytes=32 * 1024 * 1024),
+    )(*(pltpu.with_memory_space_constraint(operand, pltpu.HBM) for operand in operands))
     return result.reshape(orbitals.shape)
 
 

time: 44.1 us -> 40 us (0.907)
  Pallas kernels: 41.7 us -> 38.9 us
  local copies, waits for them, and re-layouts: 2.27 us -> 0.97 us
    pallas_call x1, Pallas kernels: 41.7 us -> 38.9 us  [body(): pl.pallas_call(kernel, out_shape=pltpu.VMEM((BOX, BOX * BOX), F32), in_sp...]
    unnamed x1, local copies, waits for them, and re-layouts: 2.27 us -> 0.97 us
where the time goes in v4:
time: 40 us; the launch traced here: 39.9 us
  Pallas kernels  38.9 us (97%)
  local copies, waits for them, and re-layouts  0.97 us (2%)
    pallas_call x1, Pallas kernels, body(): pl.pallas_call(kernel, out_shape=pltpu.VMEM((BOX, BOX * BOX), F32), in_sp...  38.9 us
    unnamed x1, local copies, waits for them, and re-layouts  0.97 us

profile of v4, /device:TPU:1, one launch (start us, length us, event | category | flops | bytes accessed | tf_op | source)
XLA Modules:
  0.0 39.9 jit_solution(3723459093702551355)
XLA Ops:
  0.0 38.9 %shard_map.55 = f32[64,4096]{1,0:T(8,128)S(1)} custom-call(bf16[64,4096]{1,0:T(8,128)(2,1)} %bitcast.4, s32[4,5]{1,0:T(4,128)} %bitcast.5, bf16[64,192]{1,0:T(8,128)(2,1)} %constant.6.clone.left_hbm, bf16[256,256]{1,0:T(8,128)(2,1)} %constant.7.clone.right_hbm, f32[33,32,128]{2,1,0:T(8,128)} %constant.8.clone.ratio_hbm), custom_call_target="tpu_custom_call" | custom-call | tf_op jit(solution)/shard_map/pallas_call | solution.py:314
  38.9 1.0 %copy.7 = f32[1,1,1,64,4096]{4,3,2,1,0:T(8,128)} copy(f32[1,1,1,64,4096]{4,3,2,1,0:T(8,128)S(1)} %bitcast.3) | data formatting | bytes 2097152

commit v5 on v4

--- a/solution.py
+++ b/solution.py
@@ -18,7 +18,7 @@
 PAD = 17
 ROWS = 4
 NEAR = 8
-GROUP = 16
+GROUP = 32
 
 
 def tables():
@@ -109,12 +109,12 @@
         return chosen
 
     barrier = pltpu.get_barrier_semaphore()
-    for device in (twin, ahead, behind):
+    for device in (ahead, behind):
         pl.semaphore_signal(barrier, inc=1, device_id=device, device_id_type=MESH)
-
-    @pl.when(here_y < span_y - 1)
-    def _():
-        pl.semaphore_signal(barrier, inc=1, device_id=beyond, device_id_type=MESH)
+    for signals, device in ((core == 1, twin), (here_y < span_y - 1, beyond)):
+        @pl.when(signals)
+        def _():
+            pl.semaphore_signal(barrier, inc=1, device_id=device, device_id_type=MESH)
 
     loads = [
         pltpu.make_async_copy(source, dest, local_sem.at[number])
@@ -127,7 +127,11 @@
     for chunk in range(CHUNKS):
         own[chunk] = orb_ref[:, chunk * LANES:(chunk + 1) * LANES]
     loads[1].wait()
-    pl.semaphore_wait(barrier, jnp.where(here_y == 0, 3, 4))
+    pl.semaphore_wait(barrier, 2 + jnp.where(core == 0, 1, 0) + jnp.where(here_y == 0, 0, 1))
+    for answers, device, number in ((core == 0, twin, 0), (here_y == span_y - 1, beyond, 1)):
+        @pl.when(answers)
+        def _():
+            pl.semaphore_signal(ready.at[number], inc=1, device_id=device, device_id_type=MESH)
 
     def box_copy(slot, source):
         return pltpu.make_async_remote_copy(
@@ -147,9 +151,19 @@
         tab_copy(slot, tab_near.at[source]).start()
         box_copy(slot, near.at[source]).start()
 
-    @pl.when(here_y == span_y - 1)
-    def _():
-        pl.semaphore_signal(ready, inc=1, device_id=beyond, device_id_type=MESH)
+    def pass_on(slot, device):
+        return [
+            pltpu.make_async_remote_copy(
+                src_ref=here.at[1], dst_ref=here.at[slot], send_sem=send.at[NEAR + slot - 6],
+                recv_sem=recv.at[slot], device_id=device, device_id_type=MESH)
+            for here, send, recv in ((tab_near, tab_send, tab_recv), (near, box_send, box_recv))
+        ]
+
+    twin_last = (here_x == 0) & (here_y == 1)
+
+    def send_twin():
+        pl.semaphore_wait(ready.at[0], 1)
+        send_own(0)
 
     @pl.when(here_y > 0)
     def _():
@@ -158,25 +172,33 @@
     @pl.when(core == 0)
     def _():
         send_own(3)
+        send_own(0)
 
     @pl.when(core == 1)
     def _():
         send_own(2)
 
-    send_own(0)
     padded[...] = jnp.zeros_like(padded)
     out_ref[...] = jnp.zeros_like(out_ref)
     padded[0, PAD:PAD + CHUNKS, HALF:HALF + BOX, :] = own[...].astype(F32)
+
+    @pl.when((core == 1) & jnp.logical_not(twin_last))
+    def _():
+        send_twin()
+
     for load in loads[2:]:
         load.wait()
 
+    hands_behind = ((core == 1) & (here_y < span_y - 1)) | (here_y == 2)
+    passes_behind = ((core == 1) & (here_y != 1)) | (here_y == 0)
     left, right = left_ref[...], right_ref[...]
     low = lax.broadcasted_iota(jnp.int32, (HALF, LANES), 1) < BOX
     me = here_x * span_y + here_y
 
     def pair(step, carry):
-        on_first = jnp.where(here_y == 0, by_step(step, (0, 3, 4, 2, 5, 1, 6, 7)), by_step(step, (0, 3, 1, 2, 4, 5, 6, 7)))
-        slot = jnp.where(core == 0, on_first, by_step(step, (0, 2, 5, 3, 1, 4, 7, 6)))
+        on_first = jnp.where(here_y == 0, by_step(step, (0, 3, 4, 1, 2, 5, 6, 7)), by_step(step, (0, 3, 1, 4, 2, 6, 5, 7)))
+        on_second = jnp.where(twin_last, by_step(step, (2, 1, 0, 5, 3, 7, 4, 6)), by_step(step, (0, 2, 5, 1, 3, 7, 4, 6)))
+        slot = jnp.where(core == 0, on_first, on_second)
         owner = pick(slot)
         other = owner[0] * span_y + owner[1]
 
@@ -192,21 +214,38 @@
 
         @pl.when((step == 1) & (here_y == 0))
         def _():
-            pl.semaphore_wait(ready, 1)
+            pl.semaphore_wait(ready.at[1], 1)
             send_own(1)
 
         tab_copy(slot, tab_here).wait_recv()
         box_copy(slot, own).wait_recv()
 
-        @pl.when(slot == 2)
+        @pl.when((slot == 2) & twin_last)
+        def _():
+            send_twin()
+
+        @pl.when((slot == 2) & hands_behind)
         def _():
             hand_on(6, 2)
-            hand_on(4, 2)
-
-        @pl.when(slot == 3)
+
+        @pl.when((slot == 3) & (core == 0))
         def _():
             hand_on(7, 3)
-            hand_on(5, 3)
+
+        for first_hop, inward in ((2, 4), (3, 5)):
+            @pl.when(slot == first_hop)
+            def _():
+                hand_on(inward, first_hop)
+
+        @pl.when((slot == 1) & (core == 0))
+        def _():
+            for copy in pass_on(7, ahead):
+                copy.start()
+
+        @pl.when((slot == 1) & passes_behind)
+        def _():
+            for copy in pass_on(6, behind):
+                copy.start()
 
         listed = jnp.int32(0)
         wanted = jnp.int32(0)
@@ -292,9 +331,22 @@
 
     for slot in range(NEAR):
         source = own if slot < 4 else near.at[2 + slot % 2]
-        tab_copy(slot, tab_here).wait_send()
-        if slot not in (2, 3):
+        if slot < 6:
+            tab_copy(slot, tab_here).wait_send()
+        if slot not in (2, 3, 6, 7):
             box_copy(slot, source).wait_send()
+
+    for holds, slot in ((hands_behind, 6), (core == 0, 7)):
+        @pl.when(holds)
+        def _():
+            tab_copy(slot, tab_here).wait_send()
+            box_copy(slot, own).wait_send()
+
+    for holds, copies in ((core == 0, pass_on(7, ahead)), (passes_behind, pass_on(6, behind))):
+        @pl.when(holds)
+        def _():
+            for copy in copies:
+                copy.wait_send()
 
     @pl.when(core == 0)
     def _():
@@ -310,7 +362,7 @@
     operands = [orbitals.reshape(BOX, BOX * BOX), pair_table.reshape(ROWS, 5)]
     operands += [jnp.asarray(table) for table in (left, right, ratios)]
     cube = (CHUNKS, BOX, LANES)
-    dma = pltpu.SemaphoreType.DMA((NEAR,))
+    dma = pltpu.SemaphoreType.DMA((NEAR + 2,))
     result = pl.pallas_call(
         kernel,
         out_shape=pltpu.VMEM((BOX, BOX * BOX), F32),
@@ -329,7 +381,7 @@
             pltpu.VMEM(cube, BF16),
             pltpu.VMEM((BOX, HALF, LANES), F32),
             dma, dma, dma, dma,
-            pltpu.SemaphoreType.REGULAR,
+            pltpu.SemaphoreType.REGULAR((2,)),
             pltpu.SemaphoreType.DMA((5,)),
         ],
         compiler_params=pltpu.CompilerParams(

time: 40 us -> 39.1 us (0.978)
  the two profiles are of different devices: /device:TPU:1 before, /device:TPU:62 now
where the time goes in v5:
time: 39.1 us; the launch traced here: 39 us
  Pallas kernels  38 us (97%)
  local copies, waits for them, and re-layouts  0.97 us (2%)
    pallas_call x1, Pallas kernels, body(): pl.pallas_call(kernel, out_shape=pltpu.VMEM((BOX, BOX * BOX), F32), in_sp...  38 us
    unnamed x1, local copies, waits for them, and re-layouts  0.97 us

profile of v5, /device:TPU:62, one launch (start us, length us, event | category | flops | bytes accessed | tf_op | source)
XLA Modules:
  0.0 39.0 jit_solution(11779340789919170287)
XLA Ops:
  0.0 38.0 %shard_map.55 = f32[64,4096]{1,0:T(8,128)S(1)} custom-call(bf16[64,4096]{1,0:T(8,128)(2,1)} %bitcast.4, s32[4,5]{1,0:T(4,128)} %bitcast.5, bf16[64,192]{1,0:T(8,128)(2,1)} %constant.6.clone.left_hbm, bf16[256,256]{1,0:T(8,128)(2,1)} %constant.7.clone.right_hbm, f32[33,32,128]{2,1,0:T(8,128)} %constant.8.clone.ratio_hbm), custom_call_target="tpu_custom_call" | custom-call | tf_op jit(solution)/shard_map/pallas_call | solution.py:366
  38.0 1.0 %copy.7 = f32[1,1,1,64,4096]{4,3,2,1,0:T(8,128)} copy(f32[1,1,1,64,4096]{4,3,2,1,0:T(8,128)S(1)} %bitcast.3) | data formatting | bytes 2097152

commit v6 on v5

--- a/solution.py
+++ b/solution.py
@@ -196,7 +196,7 @@
     me = here_x * span_y + here_y
 
     def pair(step, carry):
-        on_first = jnp.where(here_y == 0, by_step(step, (0, 3, 4, 1, 2, 5, 6, 7)), by_step(step, (0, 3, 1, 4, 2, 6, 5, 7)))
+        on_first = jnp.where(here_y == 0, jnp.where(here_x == span_x - 1, by_step(step, (0, 3, 4, 1, 2, 5, 7, 6)), by_step(step, (0, 3, 4, 1, 2, 5, 6, 7))), by_step(step, (0, 3, 1, 4, 2, 6, 5, 7)))
         on_second = jnp.where(twin_last, by_step(step, (2, 1, 0, 5, 3, 7, 4, 6)), by_step(step, (0, 2, 5, 1, 3, 7, 4, 6)))
         slot = jnp.where(core == 0, on_first, on_second)
         owner = pick(slot)

time: 39.1 us -> 37.7 us (0.964)
  the two profiles are of different devices: /device:TPU:62 before, /device:TPU:1 now
where the time goes in v6:
time: 37.7 us; the launch traced here: 37.6 us
  Pallas kernels  36.6 us (97%)
  local copies, waits for them, and re-layouts  0.97 us (3%)
    pallas_call x1, Pallas kernels, body(): pl.pallas_call(kernel, out_shape=pltpu.VMEM((BOX, BOX * BOX), F32), in_sp...  36.6 us
    unnamed x1, local copies, waits for them, and re-layouts  0.97 us

profile of v6, /device:TPU:1, one launch (start us, length us, event | category | flops | bytes accessed | tf_op | source)
XLA Modules:
  0.0 37.6 jit_solution(7842645316544616970)
XLA Ops:
  0.0 36.6 %shard_map.55 = f32[64,4096]{1,0:T(8,128)S(1)} custom-call(bf16[64,4096]{1,0:T(8,128)(2,1)} %bitcast.4, s32[4,5]{1,0:T(4,128)} %bitcast.5, bf16[64,192]{1,0:T(8,128)(2,1)} %constant.6.clone.left_hbm, bf16[256,256]{1,0:T(8,128)(2,1)} %constant.7.clone.right_hbm, f32[33,32,128]{2,1,0:T(8,128)} %constant.8.clone.ratio_hbm), custom_call_target="tpu_custom_call" | custom-call | tf_op jit(solution)/shard_map/pallas_call | solution.py:366
  36.6 1.0 %copy.7 = f32[1,1,1,64,4096]{4,3,2,1,0:T(8,128)} copy(f32[1,1,1,64,4096]{4,3,2,1,0:T(8,128)S(1)} %bitcast.3) | data formatting | bytes 2097152

commit v7 on v6

--- a/solution.py
+++ b/solution.py
@@ -28,7 +28,7 @@
     low = (sine - high.astype(np.float64)).astype(BF16)
     none = np.zeros_like(high)
     both = lambda part: np.block([[part, none], [none, part]])
-    left = np.concatenate([high, high, low], axis=1)
+    left = np.block([[high, high], [low, none]])
     right = np.block([[both(high), both(low)], [both(high), both(none)]])
     eigen = 2 - 2 * np.cos(math.pi * cells / (BOX + 1))
     row = np.arange(HALF)[:, None]
@@ -48,7 +48,8 @@
 
 def rows_dot(left, values):
     high, low = split(values)
-    return jnp.dot(left, jnp.concatenate([high, low, high], axis=0), preferred_element_type=F32)
+    both = jnp.dot(left, jnp.concatenate([high, low], axis=0), preferred_element_type=F32)
+    return both[:BOX] + both[BOX:]
 
 
 def lanes_dot(values, right):

time: 37.7 us -> 37.1 us (0.984)
  Pallas kernels: 36.6 us -> 35.8 us
    pallas_call x1, Pallas kernels: 36.6 us -> 35.8 us  [body(): pl.pallas_call(kernel, out_shape=pltpu.VMEM((BOX, BOX * BOX), F32), in_sp...]
where the time goes in v7:
time: 37.1 us; the launch traced here: 36.7 us
  Pallas kernels  35.8 us (96%)
  local copies, waits for them, and re-layouts  0.97 us (3%)
    pallas_call x1, Pallas kernels, body(): pl.pallas_call(kernel, out_shape=pltpu.VMEM((BOX, BOX * BOX), F32), in_sp...  35.8 us
    unnamed x1, local copies, waits for them, and re-layouts  0.97 us

profile of v7, /device:TPU:1, one launch (start us, length us, event | category | flops | bytes accessed | tf_op | source)
XLA Modules:
  0.0 36.7 jit_solution(376036819053817039)
XLA Ops:
  0.0 35.8 %shard_map.55 = f32[64,4096]{1,0:T(8,128)S(1)} custom-call(bf16[64,4096]{1,0:T(8,128)(2,1)} %bitcast.4, s32[4,5]{1,0:T(4,128)} %bitcast.5, bf16[128,128]{1,0:T(8,128)(2,1)} %constant.6.clone.left_hbm, bf16[256,256]{1,0:T(8,128)(2,1)} %constant.7.clone.right_hbm, f32[33,32,128]{2,1,0:T(8,128)} %constant.8.clone.ratio_hbm), custom_call_target="tpu_custom_call" | custom-call | tf_op jit(solution)/shard_map/pallas_call | solution.py:367
  35.8 1.0 %copy.7 = f32[1,1,1,64,4096]{4,3,2,1,0:T(8,128)} copy(f32[1,1,1,64,4096]{4,3,2,1,0:T(8,128)S(1)} %bitcast.3) | data formatting | bytes 2097152
